TPU v7x, 32 devices: a whole 2x2x4 slice. The times are simulated.
32 devices in a mesh: seq: 8 (over y, x, core), head: 4 (over z).
Axes of the slice: x: 2, y: 2, z: 4, core: 2. Of those that a mesh axis runs over, the one named last changes fastest.
Arguments:
- inputs: bfloat16 [16384, 1024], P(('seq', 'head')), may hold values from -6 to 6
- norm1_gain: float32 [1024], replicated, may hold values from 0.1 to 1.9
- w_query: bfloat16 [1024, 1024], P(None, 'head'), may hold values from -0.1875 to 0.1875
- w_key: bfloat16 [1024, 1024], P(None, 'head'), may hold values from -0.1875 to 0.1875
- w_value: bfloat16 [1024, 1024], P(None, 'head'), may hold values from -0.1875 to 0.1875
- w_beta: bfloat16 [1024, 8], P(None, 'head'), may hold values from -0.1875 to 0.1875
- conv_weight: float32 [3, 4, 8, 128], P(None, None, 'head'), may hold values from -3 to 3
- head_gain: float32 [128], replicated, may hold values from 0.1 to 1.9
- w_out: bfloat16 [1024, 1024], P('head'), may hold values from -0.1875 to 0.1875
- norm2_gain: float32 [1024], replicated, may hold values from 0.1 to 1.9
- w_gate: bfloat16 [1024, 2816], P(None, 'head'), may hold values from -0.1875 to 0.1875
- w_up: bfloat16 [1024, 2816], P(None, 'head'), may hold values from -0.1875 to 0.1875
- w_down: bfloat16 [2816, 1024], P('head'), may hold values from -0.109375 to 0.109375
- seq_ids: int32 [16384], P('seq'), may hold values from 0 to 4, as said below
- cotangent: bfloat16 [16384, 1024], P('seq'), may hold values from -6 to 6
Outputs:
- output: bfloat16 [16384, 1024], P(('seq', 'head'))
- inputs_grad: float32 [16384, 1024], P(('seq', 'head'))
- norm1_gain_grad: float32 [1024], replicated
- w_query_grad: float32 [1024, 1024], P('seq', 'head')
- w_key_grad: float32 [1024, 1024], P('seq', 'head')
- w_value_grad: float32 [1024, 1024], P('seq', 'head')
- w_beta_grad: float32 [1024, 8], P('seq', 'head')
- conv_weight_grad: float32 [3, 4, 8, 128], P(None, None, 'head', 'seq')
- head_gain_grad: float32 [128], replicated
- w_out_grad: float32 [1024, 1024], P('head', 'seq')
- norm2_gain_grad: float32 [1024], replicated
- w_gate_grad: float32 [1024, 2816], P('seq', 'head')
- w_up_grad: float32 [1024, 2816], P('seq', 'head')
- w_down_grad: float32 [2816, 1024], P('head', 'seq')
Inputs may be any that keep to these rules, and one draw needn't show every extreme that they name: `seq_ids`: sequence numbers never fall along the tokens and every number from 0 to 4 occurs; 4 marks the padding at the end, 1 to 512 tokens; one sequence, which one drawn from the seed, begins within the first 2048 tokens and ends within the last 2048 tokens; the others hold 1 to 256 tokens each.
All inputs are finite; a program needn't handle non-finite values.
Results may differ from a plain program's by a relative error of at most 0.023.
Values may be sent and summed in bfloat16 or wider, within the bound.
No kernel may reach another device: no remote copies, remote signals or barrier semaphores. Data moves between devices by JAX's collectives and lax.ppermute only.
A program may use at most 256 MiB of HBM per device.

v0:
```python
import jax
import jax.numpy as jnp
from jax import lax
from jax.sharding import PartitionSpec as P

BLOCK = 64
SEQS = 4


precise = lax.Precision.HIGHEST
epsilon = 1e-06
beta_shift = 4.0


def passed_along(shard, axis, by):
    count = lax.axis_size(axis)
    pairs = [(i, i + by) for i in range(count) if 0 <= i + by < count]
    return lax.ppermute(shard, axis, pairs)


def rms_scale(values, scale_gain):
    return values * lax.rsqrt(jnp.mean(values * values, -1, keepdims=True) + epsilon) * scale_gain


def unit_rows(values):
    return values * lax.rsqrt(jnp.sum(values * values, -1, keepdims=True) + epsilon)


def rounded(values):
    return lax.optimization_barrier(values.astype(jnp.bfloat16)).astype(jnp.float32)


def prepare(queries, keys_in, values_in, beta_rate, block_ids, prev_ids):
    block_len = block_ids.shape[1]
    same_seq = (block_ids[:, :, None] == block_ids[:, None, :]).astype(jnp.float32)
    carry_in = (block_ids == prev_ids[:, None]).astype(jnp.float32)
    to_last = (block_ids == block_ids[:, -1:]).astype(jnp.float32)
    row_pos = lax.broadcasted_iota(jnp.int32, (block_len, block_len), 0)
    col_pos = lax.broadcasted_iota(jnp.int32, (block_len, block_len), 1)
    strict_mask = (row_pos > col_pos).astype(jnp.float32)[None] * same_seq
    causal_mask = (row_pos >= col_pos).astype(jnp.float32)[None] * same_seq
    queries_h = jnp.transpose(queries, (0, 2, 1, 3))
    keys_h = jnp.transpose(keys_in, (0, 2, 1, 3))
    values_h = jnp.transpose(values_in, (0, 2, 1, 3))
    beta_h = jnp.transpose(beta_rate, (0, 2, 1))[..., None]
    carry_h = carry_in[:, None, :, None]
    key_scores = (
        jnp.einsum("chid,chjd->chij", keys_h, keys_h, precision=precise) * strict_mask[:, None]
    )
    system = jnp.eye(block_len, dtype=jnp.float32) + beta_h * key_scores
    right_side = jnp.concatenate([beta_h * values_h, beta_h * carry_h * keys_h], axis=-1)
    solved = lax.linalg.triangular_solve(
        system, right_side, left_side=True, lower=True, unit_diagonal=True
    )
    value_width = values_in.shape[-1]
    key_width = keys_in.shape[-1]
    pseudo = solved[..., :value_width]
    erasers = solved[..., value_width:]
    scores = (
        jnp.einsum("chid,chjd->chij", queries_h, keys_h, precision=precise) * causal_mask[:, None]
    )
    base_out = jnp.einsum("chij,chjv->chiv", scores, pseudo, precision=precise)
    reach_q = carry_h * queries_h - jnp.einsum(
        "chij,chjd->chid", scores, erasers, precision=precise
    )
    last_keys = keys_h * to_last[:, None, :, None]
    step_a = carry_in[:, -1][:, None, None, None] * jnp.eye(
        key_width, dtype=jnp.float32
    ) - jnp.einsum("chid,chie->chde", erasers, last_keys, precision=precise)
    step_b = jnp.einsum("chiv,chie->chve", pseudo, last_keys, precision=precise)
    return (base_out, reach_q, step_a, step_b)


def block_terms(queries, keys_in, values_in, beta_rate, block_ids, prev_ids):
    blocks = block_ids.shape[0]
    head_count = queries.shape[1]
    key_width = keys_in.shape[-1]
    value_width = values_in.shape[-1]
    shaped = [
        array_in.reshape(blocks, BLOCK, head_count, -1)
        for array_in in (queries, keys_in, values_in)
    ]
    base_out, reach_q, step_a, step_b = prepare(
        shaped[0],
        shaped[1],
        shaped[2],
        beta_rate.reshape(blocks, BLOCK, head_count),
        block_ids,
        prev_ids,
    )

    def compose(carried, pieces):
        acc_a, acc_b = carried
        new_a = jnp.einsum("hde,hef->hdf", acc_a, pieces[0], precision=precise)
        new_b = jnp.einsum("hvd,hde->hve", acc_b, pieces[0], precision=precise) + pieces[1]
        return ((new_a, new_b), (acc_a, acc_b))

    identity_a = jnp.broadcast_to(
        jnp.eye(key_width, dtype=jnp.float32), (head_count, key_width, key_width)
    )
    zeros_b = jnp.zeros((head_count, value_width, key_width), jnp.float32)
    totals, prefixes = lax.scan(compose, (identity_a, zeros_b), (step_a, step_b))
    return (base_out, reach_q, prefixes[0], prefixes[1], totals[0], totals[1])


def convolve(projected, rim_rows, seq_ids, rim_ids, conv_weight):
    tap_count = conv_weight.shape[1]
    length = projected.shape[0]
    kernel = jnp.transpose(conv_weight, (1, 0, 2, 3)).reshape(tap_count, -1)
    extended = jnp.concatenate([rim_rows, projected], 0)
    ext_ids = jnp.concatenate([rim_ids, seq_ids])
    summed = projected * kernel[0]
    for lag_step in range(1, tap_count):
        offset = tap_count - 1 - lag_step
        shifted = extended[offset : offset + length]
        prior_ids = ext_ids[offset : offset + length]
        summed = (
            summed
            + shifted * kernel[lag_step] * (prior_ids == seq_ids).astype(jnp.float32)[:, None]
        )
    return jax.nn.silu(summed)


def split_front(projected, rim_rows, conv_weight, seq_ids, rim_ids):
    mixed_rows = convolve(projected, rim_rows, seq_ids, rim_ids, conv_weight)
    mixed_rows = mixed_rows.reshape(
        mixed_rows.shape[0], 3, conv_weight.shape[2], conv_weight.shape[3]
    )
    return (unit_rows(mixed_rows[:, 0]), unit_rows(mixed_rows[:, 1]), mixed_rows[:, 2])


def carry_states(step_a, step_b, backward):
    direction = -1 if backward else 1

    def pass_on(outgoing):
        return passed_along(outgoing.astype(jnp.bfloat16), "seq", direction).astype(outgoing.dtype)

    def one_turn(turn_index, outgoing):
        return jnp.einsum("hvd,hde->hve", pass_on(outgoing), step_a, precision=precise) + step_b

    settled = lax.fori_loop(0, lax.axis_size("seq") - 1, one_turn, step_b)
    return pass_on(settled)


def local(
    inputs,
    norm1_gain,
    w_query,
    w_key,
    w_value,
    w_beta,
    conv_weight,
    head_gain,
    w_out,
    norm2_gain,
    w_gate,
    w_up,
    w_down,
    seq_ids,
    cotangent,
):
    own_rows = inputs.shape[0]
    head_index = lax.axis_index("head")
    tap_count = conv_weight.shape[1]
    inputs_f = inputs.astype(jnp.float32)
    normed, norm_pull = jax.vjp(rms_scale, inputs_f, norm1_gain)
    normed_block = lax.all_gather(normed.astype(jnp.bfloat16), "head", axis=0, tiled=True)
    w_proj = jnp.concatenate([w_query, w_key, w_value], 1)
    projected = jnp.dot(normed_block, w_proj, preferred_element_type=jnp.float32)
    logits = jnp.dot(normed_block, w_beta, preferred_element_type=jnp.float32)
    rim_rows, rim_marks = passed_along(
        (projected[-(tap_count - 1) :], seq_ids[-(tap_count - 1) :].astype(jnp.float32)), "seq", 1
    )
    rim_ids = rim_marks.astype(jnp.int32)
    mask_f = (seq_ids < SEQS).astype(jnp.float32)

    def front_part(proj_in, rim_in, conv_in):
        return split_front(proj_in, rim_in, conv_in, seq_ids, rim_ids)

    front_values, front_pull = jax.vjp(front_part, projected, rim_rows, conv_weight)
    queries = rounded(front_values[0])
    keys_in = rounded(front_values[1])
    values_in = rounded(front_values[2])
    gate_beta = jax.nn.sigmoid(logits - beta_shift)
    beta_rate = gate_beta * mask_f[:, None]
    length = projected.shape[0]
    blocks = length // BLOCK
    head_count = queries.shape[1]
    block_ids = seq_ids.reshape(blocks, BLOCK)
    prev_ids = jnp.concatenate([rim_ids[-1:], block_ids[:-1, -1]])

    def local_terms(query_in, key_in, value_in, rate_in):
        return block_terms(query_in, key_in, value_in, rate_in, block_ids, prev_ids)

    base_out, reach_q, prefix_a, prefix_b, total_a, total_b = local_terms(
        queries, keys_in, values_in, beta_rate
    )
    state_in = carry_states(total_a, total_b, False)
    block_states = jnp.einsum("hvd,nhde->nhve", state_in, prefix_a, precision=precise) + prefix_b
    attended_blocks = base_out + jnp.einsum(
        "nhid,nhvd->nhiv", reach_q, block_states, precision=precise
    )
    attended = jnp.transpose(attended_blocks, (0, 2, 1, 3)).reshape(length, head_count, -1)
    head_normed, head_pull = jax.vjp(rms_scale, attended, head_gain)
    head_out = (head_normed * mask_f[:, None, None]).reshape(length, -1).astype(jnp.bfloat16)
    mixer = lax.psum_scatter(
        jnp.dot(head_out, w_out, preferred_element_type=jnp.float32).astype(jnp.bfloat16),
        "head",
        scatter_dimension=0,
        tiled=True,
    ).astype(jnp.float32)
    residual = inputs_f + mixer
    normed_two, norm_two_pull = jax.vjp(rms_scale, residual, norm2_gain)
    ffn_block = lax.all_gather(normed_two.astype(jnp.bfloat16), "head", axis=0, tiled=True)
    gate_proj = jnp.dot(ffn_block, w_gate, preferred_element_type=jnp.float32)
    up_proj = jnp.dot(ffn_block, w_up, preferred_element_type=jnp.float32)
    gate_sig = jax.nn.sigmoid(gate_proj)
    gate_act = gate_proj * gate_sig
    hidden = (gate_act * up_proj).astype(jnp.bfloat16)
    ffn_out = lax.psum_scatter(
        jnp.dot(hidden, w_down, preferred_element_type=jnp.float32).astype(jnp.bfloat16),
        "head",
        scatter_dimension=0,
        tiled=True,
    ).astype(jnp.float32)
    output = (residual + ffn_out).astype(jnp.bfloat16)
    grad_rows = lax.dynamic_slice_in_dim(cotangent, head_index * own_rows, own_rows, 0).astype(
        jnp.float32
    )
    grad_down = jnp.einsum("tf,td->fd", hidden, cotangent, preferred_element_type=jnp.float32)
    grad_hidden = jnp.einsum("td,fd->tf", cotangent, w_down, preferred_element_type=jnp.float32)
    grad_gate_in = (
        grad_hidden * up_proj * (gate_sig * (1.0 + gate_proj * (1.0 - gate_sig)))
    ).astype(jnp.bfloat16)
    grad_up_in = (grad_hidden * gate_act).astype(jnp.bfloat16)
    grad_gate = jnp.einsum("td,tf->df", ffn_block, grad_gate_in, preferred_element_type=jnp.float32)
    grad_up = jnp.einsum("td,tf->df", ffn_block, grad_up_in, preferred_element_type=jnp.float32)
    grad_normed_two = lax.psum_scatter(
        (
            jnp.einsum("tf,df->td", grad_gate_in, w_gate, preferred_element_type=jnp.float32)
            + jnp.einsum("tf,df->td", grad_up_in, w_up, preferred_element_type=jnp.float32)
        ).astype(jnp.bfloat16),
        "head",
        scatter_dimension=0,
        tiled=True,
    ).astype(jnp.float32)
    grad_residual_part, grad_norm_two = norm_two_pull(grad_normed_two)
    grad_residual = grad_rows + grad_residual_part
    mixer_grad_block = lax.all_gather(
        grad_residual.astype(jnp.bfloat16), "head", axis=0, tiled=True
    )
    grad_out = jnp.einsum(
        "tc,td->cd", head_out, mixer_grad_block, preferred_element_type=jnp.float32
    )
    grad_head_out = jnp.einsum(
        "td,cd->tc", mixer_grad_block, w_out, preferred_element_type=jnp.float32
    )
    grad_head_normed = grad_head_out.reshape(length, head_count, -1) * mask_f[:, None, None]
    grad_attended, grad_head_gain = head_pull(grad_head_normed)
    grad_blocks = jnp.transpose(grad_attended.reshape(blocks, BLOCK, head_count, -1), (0, 2, 1, 3))
    grad_reach = jnp.einsum("nhiv,nhvd->nhid", grad_blocks, block_states, precision=precise)
    grad_states = jnp.einsum("nhiv,nhid->nhvd", grad_blocks, reach_q, precision=precise)
    local_grad = jnp.einsum("nhvd,nhed->hve", grad_states, prefix_a, precision=precise)
    state_out_grad = carry_states(jnp.transpose(total_a, (0, 2, 1)), local_grad, True)
    grad_prefix_a = jnp.einsum("hvd,nhve->nhde", state_in, grad_states, precision=precise)
    grad_total_a = jnp.einsum("hvd,hve->hde", state_in, state_out_grad, precision=precise)
    recomputed, terms_pull = jax.vjp(local_terms, queries, keys_in, values_in, beta_rate)
    grad_query, grad_key, grad_value, grad_beta = terms_pull(
        (grad_blocks, grad_reach, grad_prefix_a, grad_states, grad_total_a, state_out_grad)
    )
    grad_logits = (grad_beta * mask_f[:, None] * gate_beta * (1.0 - gate_beta)).astype(jnp.bfloat16)
    grad_front, grad_rim, grad_conv = front_pull((grad_query, grad_key, grad_value))
    rim_back = passed_along(grad_rim, "seq", -1)
    split_at = length - tap_count + 1
    grad_projected = jnp.concatenate(
        [grad_front[:split_at], grad_front[split_at:] + rim_back], 0
    ).astype(jnp.bfloat16)
    grad_proj_w = jnp.einsum(
        "td,tc->dc", normed_block, grad_projected, preferred_element_type=jnp.float32
    )
    column_width = w_query.shape[1]
    grad_query_w = grad_proj_w[:, :column_width]
    grad_key_w = grad_proj_w[:, column_width : 2 * column_width]
    grad_value_w = grad_proj_w[:, 2 * column_width :]
    grad_beta_w = jnp.einsum(
        "td,th->dh", normed_block, grad_logits, preferred_element_type=jnp.float32
    )
    grad_normed = lax.psum_scatter(
        (
            jnp.einsum("tc,dc->td", grad_projected, w_proj, preferred_element_type=jnp.float32)
            + jnp.einsum("th,dh->td", grad_logits, w_beta, preferred_element_type=jnp.float32)
        ).astype(jnp.bfloat16),
        "head",
        scatter_dimension=0,
        tiled=True,
    ).astype(jnp.float32)
    grad_inputs_part, grad_norm_one = norm_pull(grad_normed)
    inputs_grad = grad_residual + grad_inputs_part
    weight_sums = (
        lax.psum_scatter(
            grad_query_w.astype(jnp.bfloat16), "seq", scatter_dimension=0, tiled=True
        ).astype(jnp.float32),
        lax.psum_scatter(
            grad_key_w.astype(jnp.bfloat16), "seq", scatter_dimension=0, tiled=True
        ).astype(jnp.float32),
        lax.psum_scatter(
            grad_value_w.astype(jnp.bfloat16), "seq", scatter_dimension=0, tiled=True
        ).astype(jnp.float32),
        lax.psum_scatter(
            grad_beta_w.astype(jnp.bfloat16), "seq", scatter_dimension=0, tiled=True
        ).astype(jnp.float32),
        lax.psum_scatter(
            grad_conv.astype(jnp.bfloat16), "seq", scatter_dimension=3, tiled=True
        ).astype(jnp.float32),
        lax.psum_scatter(
            grad_out.astype(jnp.bfloat16), "seq", scatter_dimension=1, tiled=True
        ).astype(jnp.float32),
        lax.psum_scatter(
            grad_gate.astype(jnp.bfloat16), "seq", scatter_dimension=0, tiled=True
        ).astype(jnp.float32),
        lax.psum_scatter(
            grad_up.astype(jnp.bfloat16), "seq", scatter_dimension=0, tiled=True
        ).astype(jnp.float32),
        lax.psum_scatter(
            grad_down.astype(jnp.bfloat16), "seq", scatter_dimension=1, tiled=True
        ).astype(jnp.float32),
    )
    gain_sums = lax.psum((grad_norm_one, grad_norm_two, grad_head_gain), ("seq", "head"))
    return (
        output,
        inputs_grad,
        gain_sums[0],
        weight_sums[0],
        weight_sums[1],
        weight_sums[2],
        weight_sums[3],
        weight_sums[4],
        gain_sums[2],
        weight_sums[5],
        gain_sums[1],
        weight_sums[6],
        weight_sums[7],
        weight_sums[8],
    )


def solution(mesh):
    return jax.shard_map(
        local,
        mesh=mesh,
        in_specs=(
            P(("seq", "head"), None),
            P(),
            P(None, "head"),
            P(None, "head"),
            P(None, "head"),
            P(None, "head"),
            P(None, None, "head", None),
            P(),
            P("head", None),
            P(),
            P(None, "head"),
            P(None, "head"),
            P("head", None),
            P("seq"),
            P("seq", None),
        ),
        out_specs=(
            P(("seq", "head"), None),
            P(("seq", "head"), None),
            P(),
            P("seq", "head"),
            P("seq", "head"),
            P("seq", "head"),
            P("seq", "head"),
            P(None, None, "head", "seq"),
            P(),
            P("head", "seq"),
            P(),
            P("seq", "head"),
            P("seq", "head"),
            P("head", "seq"),
        ),
        check_vma=False,
    )
```

profile of v0, /device:TPU:0, one launch (start us, length us, event | category | flops | bytes accessed | tf_op | source)
XLA Modules:
  0.0 1898.9 jit_solution(7656622122849377341)
XLA Ops:
  28.1 67.0 %all-gather.4.cloned.1.call-done = bf16[2048,1024]{1,0:T(8,128)(2,1)} async-done(((bf16[512,1024]{1,0:T(8,128)(2,1)}), bf16[2048,1024]{1,0:T(8,128)(2,1)}) %all-gather.4.cloned.1.call-update) | async-done | bytes 4194320 | tf_op jit(solution)/shard_map/all_gather | solution.py:167
  110.8 17.7 fusion.32
  128.5 8.3 reshape.360
  166.0 133.9 %custom-call.10 = f32[32,2,1,64,64]{0,3,4,2,1:T(8,128)} custom-call(f32[32,2,1,64,64]{0,4,3,2,1:T(8,128)} %add_bitcast_fusion), custom_call_target="InvertDiagBlocksLowerTriangular" | custom-call | tf_op jit(solution)/shard_map/triangular_solve/custom-call.1 | solution.py:52
  312.4 8.5 fusion.53
  320.9 8.8 fusion.63
  335.3 207.8 %while.67 = (s32[]{:T(128)}, f32[2,128,128]{1,2,0:T(8,128)}, f32[2,128,128]{1,2,0:T(8,128)}, f32[32,2,128,128]{2,3,1,0:T(8,128)}, f32[32,2,128,128]{2,3,1,0:T(8,...) while((s32[]{:T(128)}, f32[2,128,128]{1,2,0:T(8,128)}, ...), condition=%wide.region_4.6_spmd.clone, body=%wide.region_3.5_spmd.clone.sunk | while | flops 100761600 | bytes 1967735 | solution.py:102
  548.0 52.3 %while.64 = (s32[]{:T(128)}, bf16[2,128,128]{2,1,0:T(8,128)(2,1)}, f32[2,128,128]{2,1,0:T(8,128)}, f32[2,128,128]{2,1,0:T(8,128)}, s32[]{:T(128)}) while((s32[]{:T(128)}, bf16[2,128,128]{2,1,0:T(8,128)(2,1)}, f32[2,128,128]{2,1,0:T(8,128)}, f32[2,128,128]{2,1,0:T(8,128)}, s32[]{:T(128)}) %tuple.145), condition=%wide.region_6.8_spmd, body=%wide.region_5.7_spmd.sunk | while | flops 50397184 | bytes 655461 | solution.py:141
  638.1 82.7 %reduce-scatter.26.cloned.1.call-done = bf16[512,1024]{1,0:T(8,128)(2,1)} async-done(((bf16[2048,1024]{1,0:T(8,128)(2,1)}), bf16[512,1024]{1,0:T(8,128)(2,1)}) %reduce-scatter.26.cloned.1.call-update) | async-done | bytes 1048592 | tf_op jit(solution)/shard_map/reduce_scatter | solution.py:206
  725.3 81.4 %all-gather.6.cloned.1.call-done = bf16[2048,1024]{1,0:T(8,128)(2,1)} async-done(((bf16[512,1024]{1,0:T(8,128)(2,1)}), bf16[2048,1024]{1,0:T(8,128)(2,1)}) %all-gather.6.cloned.1.call-update) | async-done | bytes 4194320 | tf_op jit(solution)/shard_map/all_gather | solution.py:214
  830.7 75.2 %reduce-scatter.30.cloned.1.call-done = bf16[512,1024]{1,0:T(8,128)(2,1)} async-done(((bf16[2048,1024]{1,0:T(8,128)(2,1)}), bf16[512,1024]{1,0:T(8,128)(2,1)}) %reduce-scatter.30.cloned.1.call-update) | async-done | bytes 1048592 | tf_op jit(solution)/shard_map/reduce_scatter | solution.py:238
  912.8 7.4 convolution_convert_fusion.2
  922.9 7.5 convolution_convert_fusion.3
  949.8 44.4 %all-gather.8.cloned.1.call-done = bf16[2048,1024]{1,0:T(8,128)(2,1)} async-done(((bf16[512,1024]{1,0:T(8,128)(2,1)}), bf16[2048,1024]{1,0:T(8,128)(2,1)}) %all-gather.8.cloned.1.call-update) | async-done | bytes 4194320 | tf_op jit(solution)/shard_map/all_gather | solution.py:249
  1008.6 9.5 fusion.42
  1030.2 52.9 %while.65 = (s32[]{:T(128)}, bf16[2,128,128]{2,1,0:T(8,128)(2,1)}, f32[2,128,128]{2,1,0:T(8,128)}, f32[2,128,128]{2,1,0:T(8,128)}, s32[]{:T(128)}) while((s32[]{:T(128)}, bf16[2,128,128]{2,1,0:T(8,128)(2,1)}, f32[2,128,128]{2,1,0:T(8,128)}, f32[2,128,128]{2,1,0:T(8,128)}, s32[]{:T(128)}) %tuple.187), condition=%wide.region_15.17_spmd, body=%wide.region_14.16_spmd.sunk | while | flops 50397184 | bytes 655461 | solution.py:141
  1115.8 237.3 %while.66 = (s32[]{:T(128)}, f32[2,128,128]{1,2,0:T(8,128)S(1)}, f32[2,128,128]{1,2,0:T(8,128)S(1)}, f32[32,2,128,128]{3,2,1,0:T(8,128)}, f32[32,2,128,128]{2,3,...) while((s32[]{:T(128)}, f32[2,128,128]{1,2,0:T(8,128)S(1)}, ...), condition=%wide.region_17.19_spmd, body=%wide.region_16.18_spmd.sunk | while | flops 201424896 | bytes 3278993 | solution.py:102
  1353.1 10.3 fusion.48
  1363.4 7.3 fusion.46
  1425.9 14.1 add_bitcast_fusion.2
  1447.0 25.9 %copy.397 = f32[2048,3,2,128]{3,2,1,0:T(2,128)} copy(f32[2048,3,2,128]{3,0,2,1:T(8,128)S(1)} %pad_add_fusion.1) | data formatting | bytes 12582912 | tf_op jit(solution)/shard_map/transpose(jvp())/add_any | solution.py:129
  1472.9 9.0 reshape.373
  1482.0 19.3 %multiply_reduce_fusion.3 = (f32[768]{0:T(1024)S(1)}, f32[768]{0:T(1024)S(1)}, f32[768]{0:T(1024)S(1)}, f32[768]{0:T(1024)S(1)}, f32[2048,768]{1,0:T(8,128)}) fusion(f32[2048,768]{1,0:T(8,128)} %copy-done.35, f32[3,768]{1,0:T(4,128)S(1)} %copy-done.110, f32[2048]{0:T(1024)S(1)} %copy-done.99, f32[2048]{0:T(1024)S(1)} %copy-done.97, f32[2048]{0:T(1024)S(1)} %copy-done.95, ...), kind=kLoop, calls=%fused_computation.55 | loop fusion | flops 36172800 | bytes 25211904 | tf_op jit(solution)/shard_map/transpose(jvp())/reduce_sum | solution.py:119
  1534.7 10.4 add_convert_fusion
  1562.2 15.5 reduce-scatter.42.cloned.1.call-done
  1581.9 33.1 %reduce-scatter.44.cloned.1.call-done = bf16[128,256]{1,0:T(8,128)(2,1)} async-done(((bf16[1024,256]{1,0:T(8,128)(2,1)}), bf16[128,256]{1,0:T(8,128)(2,1)}) %reduce-scatter.44.cloned.1.call-update) | async-done | bytes 65552
  1618.1 34.3 %reduce-scatter.34.cloned.1.call-done = bf16[128,256]{1,0:T(8,128)(2,1)} async-done(((bf16[1024,256]{1,0:T(8,128)(2,1)}), bf16[128,256]{1,0:T(8,128)(2,1)}) %reduce-scatter.34.cloned.1.call-update) | async-done | bytes 65552 | tf_op jit(solution)/shard_map/reduce_scatter | solution.py:300
  1653.9 36.3 %reduce-scatter.36.cloned.1.call-done = bf16[128,256]{1,0:T(8,128)(2,1)} async-done(((bf16[1024,256]{1,0:T(8,128)(2,1)}), bf16[128,256]{1,0:T(8,128)(2,1)}) %reduce-scatter.36.cloned.1.call-update) | async-done | bytes 65552 | tf_op jit(solution)/shard_map/reduce_scatter | solution.py:303
  1691.7 36.5 %reduce-scatter.38.cloned.1.call-done = bf16[128,256]{1,0:T(8,128)(2,1)} async-done(((bf16[1024,256]{1,0:T(8,128)(2,1)}), bf16[128,256]{1,0:T(8,128)(2,1)}) %reduce-scatter.38.cloned.1.call-update) | async-done | bytes 65552 | tf_op jit(solution)/shard_map/reduce_scatter | solution.py:306
  1729.7 77.4 %reduce-scatter.32.cloned.1.call-done = bf16[512,1024]{1,0:T(8,128)(2,1)} async-done(((bf16[2048,1024]{1,0:T(8,128)(2,1)}), bf16[512,1024]{1,0:T(8,128)(2,1)}) %reduce-scatter.32.cloned.1.call-update) | async-done | bytes 1048592 | tf_op jit(solution)/shard_map/reduce_scatter | solution.py:288
  1809.8 45.7 %all-reduce.12 = (f32[1024]{0:T(1024)}, f32[128]{0:T(128)}, f32[1024]{0:T(1024)}) all-reduce(f32[1024]{0:T(1024)} %get-tuple-element.550, f32[128]{0:T(128)} %get-tuple-element.544, f32[1024]{0:T(1024)} %get-tuple-element.548), channel_id=1, replica_groups=mesh['seq'=8,'head'=4] {'seq','head'}, use_global_device_ids=true, to_apply=%region_26.28 | all-reduce | flops 2176 | bytes 17408 | tf_op jit(solution)/shard_map/psum | solution.py:328
  1856.9 30.8 %reduce-scatter.28.cloned.1.call-done = bf16[512,1024]{1,0:T(8,128)(2,1)} async-done(((bf16[2048,1024]{1,0:T(8,128)(2,1)}), bf16[512,1024]{1,0:T(8,128)(2,1)}) %reduce-scatter.28.cloned.1.call-update) | async-done | bytes 1048592 | tf_op jit(solution)/shard_map/reduce_scatter | solution.py:220
  (996 shorter events, 922.1 us)
Async XLA Ops:
  7.2 87.8 %all-gather.4.cloned.1.call-start = ((), (), s32[]{:S(2)}) async-start(), calls=%async_computation.13 | async-start | bytes 5242880 | tf_op jit(solution)/shard_map/all_gather | solution.py:167
  11.4 709.4 %reduce-scatter.26.cloned.1.call-start = ((), (), s32[]{:S(2)}) async-start(), calls=%async_computation.14 | async-start | bytes 5242880 | tf_op jit(solution)/shard_map/reduce_scatter | solution.py:206
  11.6 12.8 collective-permute-start.3
  554.8 5.0 collective-permute-start
  561.6 5.9 collective-permute-start
  569.3 5.9 collective-permute-start
  577.0 5.9 collective-permute-start
  584.8 5.9 collective-permute-start
  592.5 5.9 collective-permute-start
  600.3 10.8 collective-permute-start.4
  638.1 168.5 %all-gather.6.cloned.1.call-start = ((), (), s32[]{:S(2)}) async-start(), calls=%async_computation.15 | async-start | bytes 5242880 | tf_op jit(solution)/shard_map/all_gather | solution.py:214
  725.2 180.7 %reduce-scatter.30.cloned.1.call-start = ((), (), s32[]{:S(2)}) async-start(), calls=%async_computation.17 | async-start | bytes 5242880 | tf_op jit(solution)/shard_map/reduce_scatter | solution.py:238
  830.5 163.7 %all-gather.8.cloned.1.call-start = ((), (), s32[]{:S(2)}) async-start(), calls=%async_computation.18 | async-start | bytes 5242880 | tf_op jit(solution)/shard_map/all_gather | solution.py:249
  912.8 639.6 %reduce-scatter.48.cloned.1.call-start = ((), (), s32[]{:S(2)}) async-start(), calls=%async_computation.27 | async-start | bytes 1769472
  922.9 631.4 %reduce-scatter.46.cloned.1.call-start = ((), (), s32[]{:S(2)}) async-start(), calls=%async_computation.26 | async-start | bytes 1769472
  933.1 623.1 %reduce-scatter.50.cloned.1.call-start = ((), (), s32[]{:S(2)}) async-start(), calls=%async_computation.28 | async-start | bytes 1769472
  949.7 610.0 %reduce-scatter.40.cloned.1.call-start = ((), (), s32[]{:S(2)}) async-start(), calls=%async_computation.23 | async-start | bytes 294912
  1035.6 5.3 collective-permute-start.1
  1042.7 5.9 collective-permute-start.1
  1050.4 5.9 collective-permute-start.1
  1058.2 5.9 collective-permute-start.1
  1065.9 5.9 collective-permute-start.1
  1073.6 7.7 collective-permute-start.1
  1083.1 25.5 %collective-permute-start.5 = (bf16[2,128,128]{2,1,0:T(8,128)(2,1)}, bf16[2,128,128]{2,1,0:T(8,128)(2,1)}, u32[]{:S(2)}, u32[]{:S(2)}) collective-permute-start(bf16[2,128,128]{2,1,0:T(8,128)(2,1)} %get-tuple-element.317), channel_id=1, source_target_pairs={{4,0},{8,4},{12,8},{16,12},{20,16},{24,20},{28,24},{5,1},{9,5},{13... | collective-permute-start | bytes 196616 | tf_op jit(solution)/shard_map/ppermute | solution.py:18
  1501.4 76.4 %reduce-scatter.42.cloned.1.call-start = ((), (), s32[]{:S(2)}) async-start(), calls=%async_computation.24 | async-start | bytes 36864
  1502.4 112.5 %reduce-scatter.44.cloned.1.call-start = ((), (), s32[]{:S(2)}) async-start(), calls=%async_computation.25 | async-start | bytes 589824
  1507.0 145.4 %reduce-scatter.34.cloned.1.call-start = ((), (), s32[]{:S(2)}) async-start(), calls=%async_computation.20 | async-start | bytes 589824 | tf_op jit(solution)/shard_map/reduce_scatter | solution.py:300
  1515.7 7.1 collective-permute-start.6
  1529.1 161.1 %reduce-scatter.36.cloned.1.call-start = ((), (), s32[]{:S(2)}) async-start(), calls=%async_computation.21 | async-start | bytes 589824 | tf_op jit(solution)/shard_map/reduce_scatter | solution.py:303
  1529.9 198.3 %reduce-scatter.38.cloned.1.call-start = ((), (), s32[]{:S(2)}) async-start(), calls=%async_computation.22 | async-start | bytes 589824 | tf_op jit(solution)/shard_map/reduce_scatter | solution.py:306
  1534.6 272.5 %reduce-scatter.32.cloned.1.call-start = ((), (), s32[]{:S(2)}) async-start(), calls=%async_computation.19 | async-start | bytes 5242880 | tf_op jit(solution)/shard_map/reduce_scatter | solution.py:288
  1545.1 342.6 %reduce-scatter.28.cloned.1.call-start = ((), (), s32[]{:S(2)}) async-start(), calls=%async_computation.16 | async-start | bytes 5242880 | tf_op jit(solution)/shard_map/reduce_scatter | solution.py:220
  (144 other events, 4938.2 us)
Sparse Core Ops, SparseCore 0:
  11.5 83.4 all-gather.3
  638.2 82.5 reduce-scatter.25
  725.3 81.2 all-gather.5
  830.6 75.2 reduce-scatter.29
  912.9 81.2 all-gather.7
  997.3 36.9 reduce-scatter.47
  1037.6 39.0 reduce-scatter.45
  1080.0 38.4 reduce-scatter.49
  1501.5 41.2 reduce-scatter.39
  1546.4 31.2 reduce-scatter.41
  1580.8 34.1 reduce-scatter.43
  1618.2 34.1 reduce-scatter.33
  1656.0 34.1 reduce-scatter.35
  1694.0 34.1 reduce-scatter.37
  1730.3 76.7 reduce-scatter.31
  1809.4 78.3 reduce-scatter.27
where the time goes:
time: 1910 us; the launch traced here: 1900 us
  waiting for transfers between devices  653 us (34%)
  matrix products  576 us (30%)
  other arithmetic  284 us (15%)
  local copies, waits for them, and re-layouts  264 us (14%)
  starting transfers between devices  58.2 us (3%)
  blocking collectives  45.7 us (2%)
    dot_general x96, matrix products, compose(): new_a = jnp.einsum('hde,hef->hdf', acc_a, pieces[0], precision=precise)  164 us
    dot_general x96, matrix products, compose(): jnp.einsum('hvd,hde->hve', acc_b, pieces[0], precision=precise) + pieces[1]  143 us
    another operation x5, other arithmetic, prepare(): lax.linalg.triangular_solve(system, right_side, left_side=True, lower=Tru...  140 us
    reduce_scatter x1, waiting for transfers between devices, local(): lax.psum_scatter(jnp.dot(head_out, w_out, preferred_element_type=jnp.floa...  82.7 us
    all_gather x1, waiting for transfers between devices, local(): lax.all_gather(normed_two.astype(jnp.bfloat16), 'head', axis=0, tiled=True)  81.4 us
    reduce_scatter x1, waiting for transfers between devices, local(): lax.psum_scatter((jnp.einsum('tc,dc->td', grad_projected, w_proj, preferr...  77.4 us
    reduce_scatter x1, waiting for transfers between devices, local(): lax.psum_scatter((jnp.einsum('tf,df->td', grad_gate_in, w_gate, preferred...  75.2 us
    all_gather x1, waiting for transfers between devices, local(): lax.all_gather(normed.astype(jnp.bfloat16), 'head', axis=0, tiled=True)  67 us
  transfers between devices with their start and end apart: 35, of which 27 were waited for; matrix products, arithmetic and copies ran while one was open for 31% of the time, Pallas kernels for 0%

commit v1 on v0

v1 whole, which is shorter than its diff:
```python
import functools

import jax
import jax.numpy as jnp
from jax import lax
from jax.experimental import pallas as pl
from jax.experimental.pallas import tpu as pltpu
from jax.sharding import PartitionSpec as P

SEQS = 4
CHUNK = 128
HALO = 8
epsilon = 1e-06
beta_shift = 4.0
f32 = jnp.float32
bf16 = jnp.bfloat16
WHOLE = ("seq", "head")
BY_HEAD = ("head", "seq")


def nn(a, b):
    return lax.dot_general(a, b, (((1,), (0,)), ((), ())), preferred_element_type=f32)


def nt(a, b):
    return lax.dot_general(a, b, (((1,), (1,)), ((), ())), preferred_element_type=f32)


def tn(a, b):
    return lax.dot_general(a, b, (((0,), (0,)), ((), ())), preferred_element_type=f32)


def params(mib=56, grid=1):
    return pltpu.CompilerParams(
        vmem_limit_bytes=mib << 20, dimension_semantics=("arbitrary",) * grid
    )


def lead(*shape):
    zeros = (0,) * len(shape)
    return pl.BlockSpec((None,) + shape, lambda i: (i,) + zeros)


def same(*shape):
    zeros = (0,) * len(shape)
    return pl.BlockSpec(shape, lambda i: zeros)


def sds(shape, kind):
    return jax.ShapeDtypeStruct(shape, kind)


def chunk_masks(idc_ref, idr_ref, c):
    base = HALO + c * CHUNK
    own = idc_ref[base : base + CHUNK, :]
    row = idr_ref[0:1, base : base + CHUNK]
    prev = idc_ref[base - 1 : base, :]
    last = idc_ref[base + CHUNK - 1 : base + CHUNK, :]
    equal = own == row
    carry = (own == prev).astype(f32)
    to_last = (own == last).astype(f32)
    carry_last = (last == prev).astype(f32)
    return equal, carry, to_last, carry_last


def positions():
    row = lax.broadcasted_iota(jnp.int32, (CHUNK, CHUNK), 0)
    col = lax.broadcasted_iota(jnp.int32, (CHUNK, CHUNK), 1)
    return row, col


def front_kernel(chunks, proj_ref, cw_ref, lgt_ref, idc_ref, idr_ref, qkv_ref, sum_ref, uw_ref, inv_ref, pre_ref, tot_ref):
    rows = CHUNK
    for b in range(6):
        part, hh = b // 2, b % 2
        cols = slice(b * 128, (b + 1) * 128)
        taps = [cw_ref[(part * 4 + j) * 2 + hh : (part * 4 + j) * 2 + hh + 1, :] for j in range(4)]
        for c in range(chunks):
            base = HALO + c * rows
            own = idc_ref[base : base + rows, :]
            acc = proj_ref[base : base + rows, cols] * taps[0]
            for j in range(1, 4):
                prior = idc_ref[base - j : base - j + rows, :]
                acc = acc + jnp.where(prior == own, proj_ref[base - j : base - j + rows, cols], 0.0) * taps[j]
            sum_ref[c * rows : (c + 1) * rows, cols] = acc
            mixed = acc / (1.0 + jnp.exp(-acc))
            if part < 2:
                mixed = mixed * lax.rsqrt(jnp.sum(mixed * mixed, -1, keepdims=True) + epsilon)
            qkv_ref[c * rows : (c + 1) * rows, cols] = mixed.astype(bf16)
    row, col = positions()
    differ = row ^ col
    strict = row > col
    units = [(hh, c) for c in range(chunks) for hh in range(2)]
    lower, inv, scaled = {}, {}, {}
    for hh, c in units:
        equal, carry, _, _ = chunk_masks(idc_ref, idr_ref, c)
        at = slice(c * CHUNK, (c + 1) * CHUNK)
        beta = jax.nn.sigmoid(lgt_ref[at, hh * 128 : (hh + 1) * 128] - beta_shift)
        beta = jnp.where(idc_ref[HALO + c * CHUNK : HALO + (c + 1) * CHUNK, :] < SEQS, beta, 0.0)
        keys = qkv_ref[at, 256 + hh * 128 : 256 + (hh + 1) * 128]
        values = qkv_ref[at, 512 + hh * 128 : 512 + (hh + 1) * 128]
        low = jnp.where(equal & strict, nt(keys, keys), 0.0) * beta
        lower[hh, c] = low
        inv[hh, c] = jnp.where(row == col, 1.0, 0.0) - jnp.where(differ == 1, low, 0.0)
        scaled[hh, c] = jnp.concatenate(
            [(values.astype(f32) * beta).astype(bf16), (keys.astype(f32) * (beta * carry)).astype(bf16)], axis=1
        )
    for k in range(1, 7):
        level = (differ >> k) == 1
        for u in units:
            off = jnp.where(level, lower[u], 0.0).astype(bf16)
            half = inv[u].astype(bf16)
            inv[u] = inv[u] - nn(half, nn(off, half).astype(bf16))
    for hh, c in units:
        at = slice(c * CHUNK, (c + 1) * CHUNK)
        half = inv[hh, c].astype(bf16)
        inv_ref[hh, at, :] = half
        uw_ref[hh, at, :] = nn(half, scaled[hh, c]).astype(bf16)
    eye = jnp.where(row == col, 1.0, 0.0)
    state = [[eye, jnp.zeros((CHUNK, CHUNK), f32)] for _ in range(2)]
    for c in range(chunks):
        at = slice(c * CHUNK, (c + 1) * CHUNK)
        _, _, to_last, carry_last = chunk_masks(idc_ref, idr_ref, c)
        for hh in range(2):
            packed = jnp.concatenate([state[hh][0].astype(bf16), state[hh][1].astype(bf16)], axis=1)
            pre_ref[hh, c] = packed
            moved = nn(uw_ref[hh, at, 128:256], packed)
            change = jnp.concatenate(
                [(-moved[:, :128]).astype(bf16), (uw_ref[hh, at, 0:128].astype(f32) - moved[:, 128:]).astype(bf16)], axis=1
            )
            keys = qkv_ref[at, 256 + hh * 128 : 256 + (hh + 1) * 128]
            kept = (keys.astype(f32) * to_last).astype(bf16)
            step = tn(kept, change)
            state[hh] = [state[hh][0] * carry_last + step[:, :128], state[hh][1] * carry_last + step[:, 128:]]
    for hh in range(2):
        tot_ref[hh] = jnp.concatenate([state[hh][0].astype(bf16), state[hh][1].astype(bf16)], axis=1)


def reach_kernel(chunks, qkv_ref, uw_ref, pre_ref, idc_ref, idr_ref, score_ref, reach_ref, base_ref, far_ref):
    row, col = positions()
    causal = row >= col
    for c in range(chunks):
        at = slice(c * CHUNK, (c + 1) * CHUNK)
        equal, carry, _, _ = chunk_masks(idc_ref, idr_ref, c)
        for hh in range(2):
            queries = qkv_ref[at, hh * 128 : (hh + 1) * 128]
            keys = qkv_ref[at, 256 + hh * 128 : 256 + (hh + 1) * 128]
            score = jnp.where(causal & equal, nt(queries, keys), 0.0).astype(bf16)
            score_ref[hh, at, :] = score
            both = nn(score, uw_ref[hh, at, :])
            reach = (queries.astype(f32) * carry - both[:, 128:]).astype(bf16)
            reach_ref[hh, at, :] = reach
            far = nn(reach, pre_ref[hh, c])
            far_ref[hh, at, :] = far[:, :128].astype(bf16)
            base_ref[hh, at, :] = both[:, :128] + far[:, 128:]


def attend_kernel(base_ref, far_ref, state_ref, gain_ref, idc_ref, out_ref, head_ref):
    rows = base_ref.shape[1]
    mask = (idc_ref[HALO : HALO + rows, :] < SEQS).astype(f32)
    for hh in range(2):
        out = base_ref[hh] + nn(far_ref[hh], state_ref[hh])
        out_ref[hh] = out
        rh = lax.rsqrt(jnp.mean(out * out, -1, keepdims=True) + epsilon)
        head_ref[:, hh * 128 : (hh + 1) * 128] = (out * rh * gain_ref[0:1, :] * mask).astype(bf16)


def ffn_kernel(normed_ref, dy_ref, wg_ref, wu_ref, wd_ref, out_ref, grad_ref, dg_ref, du_ref, dd_ref):
    step = pl.program_id(0)
    normed, dy = normed_ref[...], dy_ref[...]
    gate = nn(normed, wg_ref[...])
    up = nn(normed, wu_ref[...])
    sig = 1.0 / (1.0 + jnp.exp(-gate))
    act = gate * sig
    hidden = (act * up).astype(bf16)
    grad_hidden = nt(dy, wd_ref[...])
    grad_gate = (grad_hidden * up * (sig * (1.0 + gate * (1.0 - sig)))).astype(bf16)
    grad_up = (grad_hidden * act).astype(bf16)
    out = nn(hidden, wd_ref[...])
    back = nt(grad_gate, wg_ref[...]) + nt(grad_up, wu_ref[...])

    @pl.when(step == 0)
    def _():
        out_ref[...] = out
        grad_ref[...] = back

    @pl.when(step > 0)
    def _():
        out_ref[...] += out
        grad_ref[...] += back

    dd_ref[...] = tn(hidden, dy).astype(bf16)
    dg_ref[...] = tn(normed, grad_gate).astype(bf16)
    du_ref[...] = tn(normed, grad_up).astype(bf16)


def head_back_kernel(gho_ref, att_ref, far_ref, gain_ref, idc_ref, datt_ref, local_ref, gain_grad_ref):
    rows = att_ref.shape[1]
    mask = (idc_ref[HALO : HALO + rows, :] < SEQS).astype(f32)
    gain = gain_ref[0:1, :]
    total = jnp.zeros((1, 128), f32)
    for hh in range(2):
        out = att_ref[hh]
        go = gho_ref[:, hh * 128 : (hh + 1) * 128] * mask
        rh = lax.rsqrt(jnp.mean(out * out, -1, keepdims=True) + epsilon)
        total = total + jnp.sum(go * out * rh, 0, keepdims=True)
        inner = jnp.mean(out * gain * go, -1, keepdims=True)
        grad = (rh * gain * go - out * (rh * rh * rh) * inner).astype(bf16)
        datt_ref[hh] = grad
        local_ref[hh] = tn(far_ref[hh], grad).astype(bf16)
    gain_grad_ref[...] = jnp.broadcast_to(total, (8, 128))


def inner_back_kernel(chunks, qkv_ref, uw_ref, pre_ref, score_ref, datt_ref, state_ref, idc_ref, idr_ref, states_ref, pseudo_ref, dq_ref, dk_ref, dp_ref):
    row, col = positions()
    causal = row >= col
    for c in range(chunks):
        at = slice(c * CHUNK, (c + 1) * CHUNK)
        equal, carry, _, _ = chunk_masks(idc_ref, idr_ref, c)
        for hh in range(2):
            queries = qkv_ref[at, hh * 128 : (hh + 1) * 128]
            keys = qkv_ref[at, 256 + hh * 128 : 256 + (hh + 1) * 128]
            grad = datt_ref[hh, at, :]
            state = (nn(pre_ref[hh, c, :, 0:128], state_ref[hh]) + pre_ref[hh, c, :, 128:256].astype(f32)).astype(bf16)
            states_ref[hh, c] = state
            pseudo = (uw_ref[hh, at, 0:128].astype(f32) - nn(uw_ref[hh, at, 128:256], state)).astype(bf16)
            pseudo_ref[hh, at, :] = pseudo
            grad_score = jnp.where(causal & equal, nt(grad, pseudo), 0.0).astype(bf16)
            dq_ref[hh, at, :] = nt(grad, state) * carry + nn(grad_score, keys)
            dk_ref[hh, at, :] = tn(grad_score, queries)
            dp_ref[hh, at, :] = tn(score_ref[hh, at, :], grad)


def outer_back_kernel(
    chunks, qkv_ref, uw_ref, inv_ref, reach_ref, datt_ref, states_ref, pseudo_ref, dq_ref, dk_ref, dp_ref,
    sum_ref, proj_ref, lgt_ref, gout_ref, cw_ref, idc_ref, idr_ref,
    gp_ref, dcw_ref, dlgt_ref, dqkv, pad,
):
    row, col = positions()
    strict = row > col
    lane = lax.broadcasted_iota(jnp.int32, (CHUNK, 128), 1)
    grad_state = [gout_ref[hh].astype(f32) for hh in range(2)]
    for c in range(chunks - 1, -1, -1):
        at = slice(c * CHUNK, (c + 1) * CHUNK)
        equal, carry, to_last, carry_last = chunk_masks(idc_ref, idr_ref, c)
        own = idc_ref[HALO + c * CHUNK : HALO + (c + 1) * CHUNK, :]
        dlgt = jnp.zeros((CHUNK, 128), f32)
        for hh in range(2):
            keys = qkv_ref[at, 256 + hh * 128 : 256 + (hh + 1) * 128]
            keys_f = keys.astype(f32)
            values = qkv_ref[at, 512 + hh * 128 : 512 + (hh + 1) * 128]
            kept = (keys_f * to_last).astype(bf16)
            packed = grad_state[hh].astype(bf16)
            push = nn(kept, packed)
            grad_state[hh] = grad_state[hh] * carry_last + tn(reach_ref[hh, at, :], datt_ref[hh, at, :]) - tn(
                uw_ref[hh, at, 128:256], push.astype(bf16)
            )
            full = (dp_ref[hh, at, :] + push).astype(bf16)
            solved = tn(inv_ref[hh, at, :], full)
            solved_h = solved.astype(bf16)
            pseudo = pseudo_ref[hh, at, :]
            gate = jax.nn.sigmoid(lgt_ref[at, hh * 128 : (hh + 1) * 128] - beta_shift)
            mask = (own < SEQS).astype(f32)
            beta = gate * mask
            back = nt(solved_h, states_ref[hh, c]) * carry
            outer = jnp.where(equal & strict, nt(solved_h, pseudo), 0.0)
            overlap = nt(keys, keys)
            rate = jnp.sum(solved * values.astype(f32) - back * keys_f - outer * overlap, -1, keepdims=True)
            dlgt = jnp.where(lane == hh, rate * mask * gate * (1.0 - gate), dlgt)
            mixed = (outer * beta).astype(bf16)
            dqkv[at, 256 + hh * 128 : 256 + (hh + 1) * 128] = (
                dk_ref[hh, at, :] + nt(pseudo, packed) * to_last - beta * back - nn(mixed, keys) - tn(mixed, keys)
            )
            dqkv[at, 512 + hh * 128 : 512 + (hh + 1) * 128] = beta * solved
            dqkv[at, hh * 128 : (hh + 1) * 128] = dq_ref[hh, at, :]
        dlgt_ref[at, :] = dlgt
    rows = CHUNK
    length = chunks * CHUNK
    for b in range(6):
        part, hh = b // 2, b % 2
        cols = slice(b * 128, (b + 1) * 128)
        taps = [cw_ref[(part * 4 + j) * 2 + hh : (part * 4 + j) * 2 + hh + 1, :] for j in range(4)]
        pad[0:HALO, :] = jnp.zeros((HALO, 128), f32)
        pad[HALO + length : 2 * HALO + length, :] = jnp.zeros((HALO, 128), f32)
        sums = [jnp.zeros((1, 128), f32) for _ in range(4)]
        for c in range(chunks):
            at = slice(c * rows, (c + 1) * rows)
            base = HALO + c * rows
            u = sum_ref[at, cols]
            sig = 1.0 / (1.0 + jnp.exp(-u))
            grad = dqkv[at, cols]
            if part < 2:
                mixed = u * sig
                r = lax.rsqrt(jnp.sum(mixed * mixed, -1, keepdims=True) + epsilon)
                grad = r * grad - mixed * ((r * r * r) * jnp.sum(mixed * grad, -1, keepdims=True))
            grad = grad * (sig * (1.0 + u * (1.0 - sig)))
            pad[base : base + rows, :] = grad
            own = idc_ref[base : base + rows, :]
            sums[0] = sums[0] + jnp.sum(grad * proj_ref[base : base + rows, cols], 0, keepdims=True)
            for j in range(1, 4):
                prior = idc_ref[base - j : base - j + rows, :]
                sums[j] = sums[j] + jnp.sum(
                    jnp.where(prior == own, proj_ref[base - j : base - j + rows, cols], 0.0) * grad, 0, keepdims=True
                )
        for j in range(4):
            dcw_ref[(part * 4 + j) * 2 + hh : (part * 4 + j) * 2 + hh + 1, :] = sums[j]
        for start, size in [(0, HALO)] + [(HALO + c * rows, rows) for c in range(chunks)]:
            own = idc_ref[start : start + size, :]
            acc = pad[start : start + size, :] * taps[0]
            for j in range(1, 4):
                later = idc_ref[start + j : start + j + size, :]
                acc = acc + jnp.where(later == own, pad[start + j : start + j + size, :], 0.0) * taps[j]
            gp_ref[start : start + size, cols] = acc


def exchange_forward(tot, n_seq, s):
    groups = tot.shape[0]
    got = lax.all_to_all(tot, "head", 0, 0, tiled=True)

    def apply(a, x):
        return jnp.einsum("hij,hjk->hik", a.astype(bf16), x.astype(bf16), preferred_element_type=f32)

    def after(second, first):
        moved = apply(second[..., :128], first)
        return jnp.concatenate([moved[..., :128], moved[..., 128:] + second[..., 128:].astype(f32)], -1)

    whole = got[0].astype(f32)
    for j in range(1, groups):
        whole = after(got[j], whole)
    eye = jnp.broadcast_to(jnp.eye(128, dtype=f32), (2, 128, 128))
    prefix = jnp.concatenate([eye, jnp.zeros((2, 128, 128), f32)], -1)
    suffix = eye
    kept = []
    k = 1
    while k < n_seq:
        mine = whole.astype(bf16)
        other = lax.ppermute(mine, "seq", [(i, i ^ k) for i in range(n_seq)])
        upper = (s & k) != 0
        first = jnp.where(upper, other, mine)
        second = jnp.where(upper, mine, other)
        kept.append((first[..., :128], suffix.astype(bf16)))
        prefix = jnp.where(upper, after(prefix, other), prefix)
        suffix = jnp.where(upper, suffix, apply(other[..., :128], suffix))
        whole = after(second, first)
        k *= 2
    state = prefix[..., 128:]
    states = [state.astype(bf16)]
    for j in range(groups - 1):
        state = apply(got[j][..., :128], state) + got[j][..., 128:].astype(f32)
        states.append(state.astype(bf16))
    back = lax.all_to_all(jnp.stack(states), "head", 0, 0, tiled=True)
    return back, got, kept


def exchange_backward(local, got, kept, n_seq, s):
    groups = local.shape[0]
    grads = lax.all_to_all(local, "head", 0, 0, tiled=True)

    def pull(a, g):
        return jnp.einsum("hij,hik->hjk", a.astype(bf16), g.astype(bf16), preferred_element_type=f32)

    whole = grads[groups - 1].astype(f32)
    for j in range(groups - 2, -1, -1):
        whole = pull(got[j][..., :128], whole) + grads[j].astype(f32)
    later = jnp.zeros_like(whole)
    k = 1
    for first_a, suffix in kept:
        mine = whole.astype(bf16)
        other = lax.ppermute(mine, "seq", [(i, i ^ k) for i in range(n_seq)])
        upper = (s & k) != 0
        later = jnp.where(upper, later, pull(suffix, other) + later)
        first = jnp.where(upper, other, mine)
        second = jnp.where(upper, mine, other)
        whole = pull(first_a, second) + first.astype(f32)
        k *= 2
    outs = [later.astype(bf16)]
    for j in range(groups - 1, 0, -1):
        later = pull(got[j][..., :128], later) + grads[j].astype(f32)
        outs.append(later.astype(bf16))
    return lax.all_to_all(jnp.stack(outs[::-1]), "head", 0, 0, tiled=True)


def local(
    inputs, norm1_gain, w_query, w_key, w_value, w_beta, conv_weight, head_gain, w_out, norm2_gain, w_gate, w_up, w_down,
    seq_ids, cotangent,
):
    n_seq, n_head = lax.axis_size("seq"), lax.axis_size("head")
    s, z = lax.axis_index("seq"), lax.axis_index("head")
    rows, width = inputs.shape
    ff = w_gate.shape[1]
    chunks = rows // CHUNK
    ext = rows + HALO
    count = n_seq * n_head
    part = width // n_seq

    def slice_of(array, size):
        return lax.dynamic_slice_in_dim(array, s * size, size, 0)

    def gathered(array):
        piece = slice_of(array, array.shape[0] // n_seq)
        full = lax.all_gather(piece, BY_HEAD, axis=0, tiled=True)
        return full.reshape((n_head,) + array.shape)

    w_proj = gathered(jnp.concatenate([w_query, w_key, w_value], 1))
    small = jnp.concatenate([conv_weight.reshape(-1, 128), w_beta.astype(f32).T.reshape(-1, 128)], 0)
    small = lax.all_gather(small, "head", axis=0)
    taps = small[:, : 24, :]
    w_beta_all = small[:, 24:, :].reshape(n_head * 2, width).astype(bf16)
    w_out_all = gathered(w_out).reshape(-1, width)
    w_gate_all = gathered(w_gate)
    w_up_all = gathered(w_up)
    w_down_all = gathered(w_down)

    before = lax.ppermute(inputs[-HALO:], WHOLE, [(i, i + 1) for i in range(count - 1)])
    ids_before = lax.ppermute(seq_ids[-HALO:], "seq", [(i, i + 1) for i in range(n_seq - 1)])
    ids_before = jnp.where(s == 0, -1, ids_before)
    ids = lax.dynamic_slice_in_dim(jnp.concatenate([ids_before, seq_ids]), z * rows, ext)
    ids_pad = jnp.concatenate([ids, jnp.full((HALO,), -2, jnp.int32)])
    idc = jnp.broadcast_to(ids_pad[:, None], (ext + HALO, 128))
    idr = jnp.broadcast_to(ids[None, :], (8, ext))
    dy = lax.dynamic_slice_in_dim(cotangent, z * rows, rows, 0)

    x_ext = jnp.concatenate([before, inputs], 0).astype(f32)
    r1_ext = lax.rsqrt(jnp.mean(x_ext * x_ext, -1, keepdims=True) + epsilon)
    normed_ext = (x_ext * r1_ext * norm1_gain).astype(bf16)
    normed = normed_ext[HALO:]
    x, r1 = x_ext[HALO:], r1_ext[HALO:]
    projected = jnp.stack([jnp.dot(normed_ext, w_proj[g], preferred_element_type=f32) for g in range(n_head)])
    beta_wide = jnp.broadcast_to(w_beta_all.reshape(n_head, 2, 1, width), (n_head, 2, 128, width)).reshape(n_head, 256, width)
    logits = jnp.einsum("td,gcd->gtc", normed, beta_wide, preferred_element_type=f32)

    idc_spec, idr_spec = same(ext + HALO, 128), same(8, ext)
    qkv, summed, uw, inverse, prefixes, totals = pl.pallas_call(
        functools.partial(front_kernel, chunks),
        grid=(n_head,),
        in_specs=[lead(ext, 768), lead(24, 128), lead(rows, 256), idc_spec, idr_spec],
        out_specs=[
            lead(rows, 768), lead(rows, 768), lead(2, rows, 256), lead(2, rows, 128), lead(2, chunks, 128, 256),
            lead(2, 128, 256),
        ],
        out_shape=[
            sds((n_head, rows, 768), bf16), sds((n_head, rows, 768), f32), sds((n_head, 2, rows, 256), bf16),
            sds((n_head, 2, rows, 128), bf16), sds((n_head, 2, chunks, 128, 256), bf16), sds((n_head, 2, 128, 256), bf16),
        ],
        compiler_params=params(),
        name="front",
    )(projected, taps, logits, idc, idr)
    state_in, got, kept = exchange_forward(totals, n_seq, s)
    score, reach, base, far = pl.pallas_call(
        functools.partial(reach_kernel, chunks),
        grid=(n_head,),
        in_specs=[lead(rows, 768), lead(2, rows, 256), lead(2, chunks, 128, 256), idc_spec, idr_spec],
        out_specs=[lead(2, rows, 128)] * 4,
        out_shape=[sds((n_head, 2, rows, 128), kind) for kind in (bf16, bf16, f32, bf16)],
        compiler_params=params(),
        name="reach",
    )(qkv, uw, prefixes, idc, idr)
    gain_rows = jnp.broadcast_to(head_gain[None, :], (8, 128))
    attended, head_out = pl.pallas_call(
        attend_kernel,
        grid=(n_head,),
        in_specs=[lead(2, rows, 128), lead(2, rows, 128), lead(2, 128, 128), same(8, 128), idc_spec],
        out_specs=[lead(2, rows, 128), pl.BlockSpec((rows, 256), lambda i: (0, i))],
        out_shape=[sds((n_head, 2, rows, 128), f32), sds((rows, n_head * 256), bf16)],
        compiler_params=params(),
        name="attend",
    )(base, far, state_in, gain_rows, idc)

    residual = x + jnp.dot(head_out, w_out_all, preferred_element_type=f32)
    r2 = lax.rsqrt(jnp.mean(residual * residual, -1, keepdims=True) + epsilon)
    normed_two = (residual * r2 * norm2_gain).astype(bf16)
    ffn_out, grad_two, grad_gate, grad_up, grad_down = pl.pallas_call(
        ffn_kernel,
        grid=(n_head,),
        in_specs=[same(rows, width), same(rows, width), lead(width, ff), lead(width, ff), lead(ff, width)],
        out_specs=[same(rows, width), same(rows, width), lead(width, ff), lead(width, ff), lead(ff, width)],
        out_shape=[
            sds((rows, width), f32), sds((rows, width), f32), sds((n_head, width, ff), bf16), sds((n_head, width, ff), bf16),
            sds((n_head, ff, width), bf16),
        ],
        compiler_params=params(60),
        name="ffn",
    )(normed_two, dy, w_gate_all, w_up_all, w_down_all)
    output = (residual + ffn_out).astype(bf16)

    grad_norm_two = jnp.sum(grad_two * residual * r2, 0)
    scaled_two = norm2_gain * grad_two
    grad_residual = dy.astype(f32) + r2 * scaled_two - residual * (r2 * r2 * r2) * jnp.mean(residual * scaled_two, -1, keepdims=True)
    grad_mixer = grad_residual.astype(bf16)
    grad_out = jnp.einsum("tc,td->cd", head_out, grad_mixer, preferred_element_type=f32).astype(bf16)
    grad_head_out = jnp.einsum("td,cd->tc", grad_mixer, w_out_all, preferred_element_type=f32)

    datt, local_grad, gain_part = pl.pallas_call(
        head_back_kernel,
        grid=(n_head,),
        in_specs=[
            pl.BlockSpec((rows, 256), lambda i: (0, i)), lead(2, rows, 128), lead(2, rows, 128), same(8, 128), idc_spec,
        ],
        out_specs=[lead(2, rows, 128), lead(2, 128, 128), lead(8, 128)],
        out_shape=[sds((n_head, 2, rows, 128), bf16), sds((n_head, 2, 128, 128), bf16), sds((n_head, 8, 128), f32)],
        compiler_params=params(),
        name="head_back",
    )(grad_head_out, attended, far, gain_rows, idc)
    grad_out_state = exchange_backward(local_grad, got, kept, n_seq, s)
    states, pseudo, dq, dk, dp = pl.pallas_call(
        functools.partial(inner_back_kernel, chunks),
        grid=(n_head,),
        in_specs=[
            lead(rows, 768), lead(2, rows, 256), lead(2, chunks, 128, 256), lead(2, rows, 128), lead(2, rows, 128),
            lead(2, 128, 128), idc_spec, idr_spec,
        ],
        out_specs=[lead(2, chunks, 128, 128)] + [lead(2, rows, 128)] * 4,
        out_shape=[sds((n_head, 2, chunks, 128, 128), bf16)]
        + [sds((n_head, 2, rows, 128), kind) for kind in (bf16, f32, f32, f32)],
        compiler_params=params(),
        name="inner_back",
    )(qkv, uw, prefixes, score, datt, state_in, idc, idr)
    gp_ext, grad_taps, grad_logits = pl.pallas_call(
        functools.partial(outer_back_kernel, chunks),
        grid=(n_head,),
        in_specs=[
            lead(rows, 768), lead(2, rows, 256), lead(2, rows, 128), lead(2, rows, 128), lead(2, rows, 128),
            lead(2, chunks, 128, 128), lead(2, rows, 128), lead(2, rows, 128), lead(2, rows, 128), lead(2, rows, 128),
            lead(rows, 768), lead(ext, 768), lead(rows, 256), lead(2, 128, 128), lead(24, 128), idc_spec, idr_spec,
        ],
        out_specs=[lead(ext, 768), lead(24, 128), lead(rows, 128)],
        out_shape=[sds((n_head, ext, 768), f32), sds((n_head, 24, 128), f32), sds((n_head, rows, 128), f32)],
        scratch_shapes=[pltpu.VMEM((rows, 768), f32), pltpu.VMEM((rows + 2 * HALO, 128), f32)],
        compiler_params=params(),
        name="outer_back",
    )(
        qkv, uw, inverse, reach, datt, states, pseudo, dq, dk, dp, summed, projected, logits, grad_out_state, taps, idc, idr,
    )

    from_next = lax.ppermute(gp_ext[:, :HALO], WHOLE, [(i + 1, i) for i in range(count - 1)])
    grad_proj = jnp.concatenate([gp_ext[:, HALO:rows], gp_ext[:, rows:] + from_next], 1).astype(bf16)
    grad_logits = jnp.concatenate([grad_logits[g, :, :2] for g in range(n_head)], 1).astype(bf16)
    grad_w = jnp.stack([
        jnp.einsum("td,tc->dc", normed, grad_proj[g], preferred_element_type=f32).astype(bf16) for g in range(n_head)
    ])
    grad_beta_w = jnp.einsum("td,th->hd", normed, grad_logits, preferred_element_type=f32)
    grad_normed = jnp.dot(grad_logits, w_beta_all, preferred_element_type=f32)
    for g in range(n_head):
        grad_normed = grad_normed + jnp.einsum("tc,dc->td", grad_proj[g], w_proj[g], preferred_element_type=f32)

    def scattered(array):
        return lax.psum_scatter(array.reshape((-1,) + array.shape[3:]), BY_HEAD, scatter_dimension=0, tiled=True).astype(f32)

    tap_pieces = grad_taps.reshape(n_head, 24, n_seq, 128 // n_seq).transpose(0, 2, 1, 3).reshape(n_head, n_seq, -1)
    beta_pieces = grad_beta_w.reshape(n_head, 2, n_seq, part).transpose(0, 2, 1, 3).reshape(n_head, n_seq, -1)
    extra = jnp.concatenate([tap_pieces, beta_pieces], -1).astype(bf16)
    extra_size = extra.shape[-1]
    extra_rows = -(-extra_size // 768)
    extra_rows = -(-extra_rows // 8) * 8
    extra = jnp.pad(extra, ((0, 0), (0, 0), (0, extra_rows * 768 - extra_size))).reshape(n_head, n_seq, extra_rows, 768)
    sum_w = scattered(jnp.concatenate([grad_w.reshape(n_head, n_seq, part, 768), extra], 2))
    sum_gate = scattered(grad_gate.reshape(n_head, n_seq, part, ff))
    sum_up = scattered(grad_up.reshape(n_head, n_seq, part, ff))
    sum_down = scattered(grad_down.reshape(n_head, ff, n_seq, part).transpose(0, 2, 1, 3))
    sum_out = scattered(grad_out.reshape(n_head, 256, n_seq, part).transpose(0, 2, 1, 3))
    flat = sum_w[part:].reshape(-1)
    tap_size = 24 * (128 // n_seq)
    sum_taps = flat[:tap_size].reshape(3, 4, 2, 128 // n_seq)
    sum_beta = flat[tap_size : tap_size + 2 * part].reshape(2, part).T

    grad_norm_one = jnp.sum(grad_normed * x * r1, 0)
    scaled_one = norm1_gain * grad_normed
    inputs_grad = grad_residual + r1 * scaled_one - x * (r1 * r1 * r1) * jnp.mean(x * scaled_one, -1, keepdims=True)
    gains = lax.psum((grad_norm_one, grad_norm_two, jnp.sum(gain_part[:, 0], 0)), WHOLE)
    return (
        output, inputs_grad, gains[0], sum_w[:part, :256], sum_w[:part, 256:512], sum_w[:part, 512:], sum_beta, sum_taps, gains[2],
        sum_out, gains[1], sum_gate, sum_up, sum_down,
    )


def solution(mesh):
    return jax.shard_map(
        local,
        mesh=mesh,
        in_specs=(
            P(("seq", "head"), None),
            P(),
            P(None, "head"),
            P(None, "head"),
            P(None, "head"),
            P(None, "head"),
            P(None, None, "head", None),
            P(),
            P("head", None),
            P(),
            P(None, "head"),
            P(None, "head"),
            P("head", None),
            P("seq"),
            P("seq", None),
        ),
        out_specs=(
            P(("seq", "head"), None),
            P(("seq", "head"), None),
            P(),
            P("seq", "head"),
            P("seq", "head"),
            P("seq", "head"),
            P("seq", "head"),
            P(None, None, "head", "seq"),
            P(),
            P("head", "seq"),
            P(),
            P("seq", "head"),
            P("seq", "head"),
            P("head", "seq"),
        ),
        check_vma=False,
    )
```

time: 1910 us -> 1080 us (0.57)
  matrix products: 576 us -> 38.6 us
  other arithmetic: 284 us -> 33.1 us
  local copies, waits for them, and re-layouts: 264 us -> 55 us
  Pallas kernels: 0 us -> 124 us
  blocking collectives: 45.7 us -> 94 us
  starting transfers between devices: 58.2 us -> 24 us
  waiting for transfers between devices: 653 us -> 683 us
    dot_general x250 -> x40, matrix products: 562 us -> 38.6 us  [the longest x4 9.9 us: local(): jnp.einsum('tc,dc->td', grad_proj[g], w_proj[g], preferred_element_type=f32)]
    unnamed x22 -> x12, waiting for transfers between devices: 49.6 us -> 195 us
    another operation x6 -> x12, other arithmetic: 140 us -> 6.8 us  [the longest x1 2.98 us: local(): jnp.stack([jnp.dot(normed_ext, w_proj[g], preferred_element_type=f32) for...]
    pallas_call x0 -> x7, Pallas kernels: none -> 124 us  [the longest x1 37.2 us: local(): pl.pallas_call(ffn_kernel, grid=(n_head,), in_specs=[same(rows, width), s...]
    reduce_scatter x7 -> x3, waiting for transfers between devices: 373 us -> 263 us  [scattered(): lax.psum_scatter(array.reshape((-1,) + array.shape[3:]), BY_HEAD, scatter...]
    while x131 -> x0, local copies, waits for them, and re-layouts: 62.8 us -> none
    ppermute x19 -> x9, starting transfers between devices: 57.1 us -> 13.3 us  [the longest x1 4.31 us: local(): lax.ppermute(inputs[-HALO:], WHOLE, [(i, i + 1) for i in range(count - 1)])]
    all_to_all x0 -> x2, blocking collectives: none -> 39.5 us  [the longest x1 26 us: exchange_forward(): got = lax.all_to_all(tot, 'head', 0, 0, tiled=True)]
  transfers between devices with their start and end apart: 35 -> 21, of which waited for: 27 -> 15; matrix products, arithmetic and copies ran while one was open for 31% -> 10% of each run, Pallas kernels for 0% -> 8%
where the time goes in v1:
time: 1080 us; the launch traced here: 1070 us
  waiting for transfers between devices  683 us (63%)
  Pallas kernels  124 us (11%)
  blocking collectives  94 us (9%)
  local copies, waits for them, and re-layouts  55 us (5%)
  matrix products  38.6 us (4%)
  other arithmetic  33.1 us (3%)
  starting transfers between devices  24 us (2%)
  between operations  15.9 us (1%)
    reduce_scatter x3, waiting for transfers between devices, scattered(): lax.psum_scatter(array.reshape((-1,) + array.shape[3:]), BY_HEAD, scatter...  263 us
    all_gather x5, waiting for transfers between devices, gathered(): full = lax.all_gather(piece, BY_HEAD, axis=0, tiled=True)  208 us
    unnamed x12, waiting for transfers between devices  195 us
    psum x1, blocking collectives, local(): lax.psum((grad_norm_one, grad_norm_two, jnp.sum(gain_part[:, 0], 0)), WHOLE)  40.9 us
    pallas_call x1, Pallas kernels, local(): pl.pallas_call(ffn_kernel, grid=(n_head,), in_specs=[same(rows, width), s...  37.2 us
    pallas_call x1, Pallas kernels, local(): pl.pallas_call(functools.partial(outer_back_kernel, chunks), grid=(n_head...  26.5 us
    all_to_all x1, blocking collectives, exchange_forward(): got = lax.all_to_all(tot, 'head', 0, 0, tiled=True)  26 us
    pallas_call x1, Pallas kernels, local(): pl.pallas_call(functools.partial(front_kernel, chunks), grid=(n_head,), i...  22.2 us
  transfers between devices with their start and end apart: 21, of which 15 were waited for; matrix products, arithmetic and copies ran while one was open for 10% of the time, Pallas kernels for 8%

profile of v1, /device:TPU:0, one launch (start us, length us, event | category | flops | bytes accessed | tf_op | source)
XLA Modules:
  0.0 1068.2 jit_solution(9971851116895245953)
XLA Ops:
  17.3 4.3 collective-permute-start
  21.7 13.6 %all-gather = f32[160,128]{1,0:T(8,128)S(1)} all-gather(f32[40,128]{1,0:T(8,128)S(1)} %pad_maximum_fusion.9), channel_id=2, replica_groups=mesh['seq'=8,'head'=4] {'head'}, dimensions={0}, use_global_device_ids=true | all-gather | bytes 102400 | tf_op jit(solution)/shard_map/all_gather | solution.py:406
  40.2 44.0 %all-gather.7.cloned.1.call-done = bf16[4096,768]{1,0:T(8,128)(2,1)} async-done(((bf16[128,768]{1,0:T(8,128)(2,1)}), bf16[4096,768]{1,0:T(8,128)(2,1)}) %all-gather.7.cloned.1.call-update) | async-done | bytes 6291472 | tf_op jit(solution)/shard_map/all_gather | solution.py:401
  94.9 22.2 %front.1 = (bf16[4,512,768]{2,1,0:T(8,128)(2,1)}, f32[4,512,768]{2,1,0:T(8,128)}, bf16[4,2,512,256]{3,2,1,0:T(8,128)(2,1)}, bf16[4,2,512,128]{3,2,1,0:T(8,128)(2...) custom-call(f32[4,520,768]{2,1,0:T(8,128)} %pad_maximum_fusion.1.proj_ref, ...), custom_call_target="tpu_custom_call" | custom-call | tf_op jit(solution)/shard_map/front/pallas_call | solution.py:433
  117.2 26.0 %all_to_all.20 = bf16[4,2,128,256]{3,2,1,0:T(8,128)(2,1)S(1)} all-to-all(bf16[4,2,128,256]{3,2,1,0:T(8,128)(2,1)} %get-tuple-element.47), channel_id=1, replica_groups=mesh['seq'=8,'head'=4] {'head'}, dimensions={0} | all-to-all | bytes 1048576 | tf_op jit(solution)/shard_map/all_to_all | solution.py:318
  148.1 3.9 collective-permute-done.3
  154.4 3.3 collective-permute-done.4
  159.2 6.6 all-to-all-start.1
  169.7 8.3 copy.63
  178.0 65.9 %all-gather.11.cloned.1.call-done = bf16[4096,704]{0,1:T(8,128)(2,1)} async-done(((bf16[128,704]{0,1:T(8,128)(2,1)}), bf16[4096,704]{0,1:T(8,128)(2,1)}) %all-gather.11.cloned.1.call-update) | async-done | bytes 5767184 | tf_op jit(solution)/shard_map/all_gather | solution.py:401
  243.9 8.5 copy.62
  252.4 9.1 reach.1
  262.2 4.8 attend.1
  267.0 34.3 %all-gather.9.cloned.1.call-done = bf16[1024,1024]{1,0:T(8,128)(2,1)} async-done(((bf16[32,1024]{1,0:T(8,128)(2,1)}), bf16[1024,1024]{1,0:T(8,128)(2,1)}) %all-gather.9.cloned.1.call-update) | async-done | bytes 2097168 | tf_op jit(solution)/shard_map/all_gather | solution.py:401
  301.2 3.9 multiply_reduce_fusion.5
  306.4 63.7 %all-gather.15.cloned.1.call-done = bf16[2816,1024]{1,0:T(8,128)(2,1)} async-done(((bf16[88,1024]{1,0:T(8,128)(2,1)}), bf16[2816,1024]{1,0:T(8,128)(2,1)}) %all-gather.15.cloned.1.call-update) | async-done | bytes 5767184 | tf_op jit(solution)/shard_map/all_gather | solution.py:401
  370.1 37.2 %ffn.1 = (f32[512,1024]{1,0:T(8,128)}, f32[512,1024]{1,0:T(8,128)}, bf16[4,1024,704]{2,1,0:T(8,128)(2,1)}, bf16[4,1024,704]{2,1,0:T(8,128)(2,1)}, bf16[4,704,1024]{2,1,0:T(8,128)(2,1)}) custom-call(bf16[512,1024]{1,0:T(8,128)(2,1)} %multiply_convert_fusion.1.normed_ref, bf16[512,1024]{1,0:T(8,128)(2,1)} %constant_dynamic-slice_fusion.3.dy_ref, ...), custom_call_target="tpu_custom_call" | custom-call | tf_op jit(solution)/shard_map/ffn/pallas_call | solution.py:472
  419.6 4.2 fusion.41.gho_ref
  423.8 5.5 head_back.1
  429.3 13.5 %all_to_all.21 = bf16[4,2,128,128]{3,2,1,0:T(8,128)(2,1)S(1)} all-to-all(bf16[4,2,128,128]{3,2,1,0:T(8,128)(2,1)} %get-tuple-element.62), channel_id=1, replica_groups=mesh['seq'=8,'head'=4] {'head'}, dimensions={0} | all-to-all | bytes 524288 | tf_op jit(solution)/shard_map/all_to_all | solution.py:357
  455.9 3.4 all-to-all-start.3
  459.3 19.2 %inner_back.1 = (bf16[4,2,4,128,128]{4,3,2,1,0:T(8,128)(2,1)}, bf16[4,2,512,128]{3,2,1,0:T(8,128)(2,1)}, f32[4,2,512,128]{3,2,1,0:T(8,128)}, f32[4,2,512,128]{3,2,1,0:T(8,128)}, f32[4,2,512,128]{3,2,1,0:T(8,128)}) custom-call(bf16[4,512,768]{2,1,0:T(8,128)(2,1)} %get-tuple-element.42.qkv_ref, bf16[4,2,512,256]{3,2,1,0:T(8,128)(2,1)} %get-tuple-element.43.uw_ref, ...), custom_call_target="tpu_custom_call" | custom-call | tf_op jit(solution)/shard_map/inner_back/pallas_call | solution.py:505
  479.3 26.5 %outer_back.1 = (f32[4,520,768]{2,1,0:T(8,128)}, f32[4,24,128]{2,1,0:T(8,128)}, f32[4,512,128]{2,1,0:T(8,128)}) custom-call(bf16[4,512,768]{2,1,0:T(8,128)(2,1)} %get-tuple-element.42.qkv_ref, bf16[4,2,512,256]{3,2,1,0:T(8,128)(2,1)} %get-tuple-element.43.uw_ref, bf16[4,2,512,128]{3,2,1,0:T(8,128)(2,1)} %get-tuple-element.51.inv_ref, ...), custom_call_target="tpu_custom_call" | custom-call | tf_op jit(solution)/shard_map/outer_back/pallas_call | solution.py:518
  521.5 3.3 pad_maximum_fusion
  525.1 4.1 copy.103
  529.6 3.8 copy.84
  548.6 40.9 %all-reduce.3 = (f32[1024]{0:T(1024)}, f32[128]{0:T(128)}, f32[1024]{0:T(1024)}) all-reduce(f32[1024]{0:T(1024)S(1)} %get-tuple-element.70, f32[128]{0:T(128)S(1)} %copy-done.56, f32[1024]{0:T(1024)S(1)} %copy-done.52), channel_id=1, replica_groups=mesh['seq'=8,'head'=4] {'seq','head'}, use_global_device_ids=true, to_apply=%region_5.6 | all-reduce | flops 2176 | bytes 17408 | tf_op jit(solution)/shard_map/psum | solution.py:569
  589.6 4.3 multiply_subtract_fusion
  595.4 75.5 %reduce-scatter.18.cloned.1.call-done = bf16[128,704]{1,0:T(8,128)(2,1)} async-done(((bf16[4096,704]{1,0:T(8,128)(2,1)}), bf16[128,704]{1,0:T(8,128)(2,1)}) %reduce-scatter.18.cloned.1.call-update) | async-done | bytes 180240
  672.8 117.6 %reduce-scatter.16.cloned.1.call-done = bf16[128,704]{1,0:T(8,128)(2,1)} async-done(((bf16[4096,704]{1,0:T(8,128)(2,1)}), bf16[128,704]{1,0:T(8,128)(2,1)}) %reduce-scatter.16.cloned.1.call-update) | async-done | bytes 180240
  792.2 121.4 %reduce-scatter.10.cloned.1.call-done = bf16[136,768]{1,0:T(8,128)(2,1)} async-done(((bf16[4352,768]{1,0:T(8,128)(2,1)}), bf16[136,768]{1,0:T(8,128)(2,1)}) %reduce-scatter.10.cloned.1.call-update) | async-done | bytes 208912 | tf_op jit(solution)/shard_map/reduce_scatter | solution.py:547
  917.4 141.8 %reduce-scatter.14.cloned.1.call-done = bf16[704,128]{1,0:T(8,128)(2,1)} async-done(((bf16[22528,128]{1,0:T(8,128)(2,1)}), bf16[704,128]{1,0:T(8,128)(2,1)}) %reduce-scatter.14.cloned.1.call-update) | async-done | bytes 180240 | tf_op jit(solution)/shard_map/reduce_scatter | solution.py:547
  (288 shorter events, 107.7 us)
Async XLA Ops:
  7.2 77.0 %all-gather.7.cloned.1.call-start = ((), (), s32[]{:S(2)}) async-start(), calls=%async_computation.9 | async-start | bytes 6488064 | tf_op jit(solution)/shard_map/all_gather | solution.py:401
  9.1 160.6 %all-gather.13.cloned.1.call-start = ((), (), s32[]{:S(2)}) async-start(), calls=%async_computation.12 | async-start | bytes 5947392 | tf_op jit(solution)/shard_map/all_gather | solution.py:401
  9.9 234.0 %all-gather.11.cloned.1.call-start = ((), (), s32[]{:S(2)}) async-start(), calls=%async_computation.11 | async-start | bytes 5947392 | tf_op jit(solution)/shard_map/all_gather | solution.py:401
  11.6 289.7 %all-gather.9.cloned.1.call-start = ((), (), s32[]{:S(2)}) async-start(), calls=%async_computation.10 | async-start | bytes 2162688 | tf_op jit(solution)/shard_map/all_gather | solution.py:401
  13.1 357.0 %all-gather.15.cloned.1.call-start = ((), (), s32[]{:S(2)}) async-start(), calls=%async_computation.13 | async-start | bytes 5947392 | tf_op jit(solution)/shard_map/all_gather | solution.py:401
  14.9 21.0 %collective-permute-start.1 = (s32[8]{0:T(128)S(1)}, s32[8]{0:T(128)S(1)}, u32[]{:S(2)}, u32[]{:S(2)}) collective-permute-start(s32[8]{0:T(128)S(1)} %slice.287), channel_id=1, source_target_pairs={{0,4},{4,8},{8,12},{12,16},{16,20},{20,24},{24,28},{1,5},{5,9},{9,... | collective-permute-start | bytes 104 | tf_op jit(solution)/shard_map/ppermute | solution.py:415
  17.3 18.7 %collective-permute-start = (bf16[8,1024]{1,0:T(8,128)(2,1)S(1)}, bf16[8,1024]{1,0:T(8,128)(2,1)S(1)}, u32[]{:S(2)}, u32[]{:S(2)}) collective-permute-start(bf16[8,1024]{1,0:T(8,128)(2,1)S(1)} %slice.278), channel_id=1, source_target_pairs={{0,1},{1,2},{2,3},{3,4},{4,5},{5,6},{6,7},{7,8},{8,9},{9,10},{10,1... | collective-permute-start | bytes 49160 | tf_op jit(solution)/shard_map/ppermute | solution.py:414
  37.3 470.3 %copy-start.8 = (bf16[520,1024]{1,0:T(8,128)(2,1)}, bf16[520,1024]{1,0:T(8,128)(2,1)S(1)}, u32[]{:S(2)}) copy-start(bf16[520,1024]{1,0:T(8,128)(2,1)S(1)} %multiply_convert_fusion) | copy-start | bytes 3194884
  144.6 1.4 collective-permute-start.2
  146.3 5.6 collective-permute-start.3
  152.7 5.1 collective-permute-start.4
  159.2 102.2 %all-to-all-start.1 = ((bf16[4,2,128,128]{3,2,1,0:T(8,128)(2,1)}), bf16[4,2,128,128]{3,2,1,0:T(8,128)(2,1)S(1)}, u32[]{:S(2)}, u32[]{:S(2)}) async-start(bf16[4,2,128,128]{3,2,1,0:T(8,128)(2,1)} %pad_maximum_fusion.3), calls=%async_computation.1 | async-start | bytes 524288 | tf_op jit(solution)/shard_map/all_to_all | solution.py:351
  165.8 428.1 %reduce-scatter.12.cloned.1.call-start = ((), (), s32[]{:S(2)}) async-start(), calls=%async_computation.15 | async-start | bytes 2162688 | tf_op jit(solution)/shard_map/reduce_scatter | solution.py:547
  417.2 253.7 %reduce-scatter.18.cloned.1.call-start = ((), (), s32[]{:S(2)}) async-start(), calls=%async_computation.18 | async-start | bytes 6488064
  417.9 372.4 %reduce-scatter.16.cloned.1.call-start = ((), (), s32[]{:S(2)}) async-start(), calls=%async_computation.17 | async-start | bytes 6488064
  423.8 19.2 %copy-start.37 = (bf16[2,128,256]{2,1,0:T(8,128)(2,1)S(1)}, bf16[2,128,256]{2,1,0:T(8,128)(2,1)}, u32[]{:S(2)}) copy-start(bf16[2,128,256]{2,1,0:T(8,128)(2,1)} %get-tuple-element.83) | copy-start | bytes 393220
  423.8 19.7 %copy-start.17 = (bf16[2,128,256]{2,1,0:T(8,128)(2,1)S(1)}, bf16[2,128,256]{2,1,0:T(8,128)(2,1)}, u32[]{:S(2)}) copy-start(bf16[2,128,256]{2,1,0:T(8,128)(2,1)} %copy-done.16) | copy-start | bytes 393220
  423.8 19.7 %copy-start.27 = (f32[128,128]{1,0:T(8,128)S(1)}, f32[128,128]{1,0:T(8,128)}, u32[]{:S(2)}) copy-start(f32[128,128]{1,0:T(8,128)} %copy-done.26) | copy-start | bytes 196612
  423.8 19.7 %copy-start.33 = (bf16[128,128]{1,0:T(8,128)(2,1)S(1)}, bf16[128,128]{1,0:T(8,128)(2,1)}, u32[]{:S(2)}) copy-start(bf16[128,128]{1,0:T(8,128)(2,1)} %copy-done.32) | copy-start | bytes 98308
  423.8 20.9 %copy-start.29 = (bf16[2,128,256]{2,1,0:T(8,128)(2,1)S(1)}, bf16[2,128,256]{2,1,0:T(8,128)(2,1)}, u32[]{:S(2)}) copy-start(bf16[2,128,256]{2,1,0:T(8,128)(2,1)} %copy-done.28) | copy-start | bytes 393220
  423.8 25.5 %copy-start.31 = (bf16[2,128,256]{2,1,0:T(8,128)(2,1)S(1)}, bf16[2,128,256]{2,1,0:T(8,128)(2,1)}, u32[]{:S(2)}) copy-start(bf16[2,128,256]{2,1,0:T(8,128)(2,1)} %copy-done.30) | copy-start | bytes 393220
  429.3 24.8 %copy-start.19 = (bf16[2,128,256]{2,1,0:T(8,128)(2,1)S(1)}, bf16[2,128,256]{2,1,0:T(8,128)(2,1)}, u32[]{:S(2)}) copy-start(bf16[2,128,256]{2,1,0:T(8,128)(2,1)} %copy-done.18) | copy-start | bytes 393220
  429.3 25.2 %copy-start.23 = (bf16[2,128,256]{2,1,0:T(8,128)(2,1)S(1)}, bf16[2,128,256]{2,1,0:T(8,128)(2,1)}, u32[]{:S(2)}) copy-start(bf16[2,128,256]{2,1,0:T(8,128)(2,1)} %copy-done.22) | copy-start | bytes 393220
  443.4 1.3 collective-permute-start.5
  444.9 4.3 collective-permute-start.6
  449.5 4.6 collective-permute-start.7
  455.9 22.7 %all-to-all-start.3 = ((bf16[4,2,128,128]{3,2,1,0:T(8,128)(2,1)}), bf16[4,2,128,128]{3,2,1,0:T(8,128)(2,1)S(1)}, u32[]{:S(2)}, u32[]{:S(2)}) async-start(bf16[4,2,128,128]{3,2,1,0:T(8,128)(2,1)} %pad_maximum_fusion.4), calls=%async_computation.3 | async-start | bytes 524288 | tf_op jit(solution)/shard_map/all_to_all | solution.py:380
  459.3 454.3 %reduce-scatter.10.cloned.1.call-start = ((), (), s32[]{:S(2)}) async-start(), calls=%async_computation.14 | async-start | bytes 6893568 | tf_op jit(solution)/shard_map/reduce_scatter | solution.py:547
  509.8 6.5 collective-permute-start.8
  524.8 534.4 %reduce-scatter.14.cloned.1.call-start = ((), (), s32[]{:S(2)}) async-start(), calls=%async_computation.16 | async-start | bytes 5947392 | tf_op jit(solution)/shard_map/reduce_scatter | solution.py:547
  546.2 43.4 %copy-start.7 = (f32[512,1024]{1,0:T(8,128)S(1)}, f32[512,1024]{1,0:T(8,128)}, u32[]{:S(2)}) copy-start(f32[512,1024]{1,0:T(8,128)} %copy-done.5) | copy-start | bytes 6291460
  589.6 471.3 %copy-start.1 = (bf16[1024,704]{0,1:T(8,128)(2,1)S(1)}, bf16[1024,704]{0,1:T(8,128)(2,1)}, u32[]{:S(2)}) copy-start(bf16[1024,704]{0,1:T(8,128)(2,1)} %param.26) | copy-start | bytes 4325380
  (48 other events, 242.2 us)
Sparse Core Ops, SparseCore 0:
  11.5 72.6 all-gather.6
  87.1 78.4 all-gather.12
  169.1 74.7 all-gather.10
  246.6 54.5 all-gather.8
  303.9 66.1 all-gather.14
  417.3 136.3 reduce-scatter.11
  560.3 110.6 reduce-scatter.17
  676.6 113.7 reduce-scatter.15
  797.0 116.5 reduce-scatter.9
  915.8 143.3 reduce-scatter.13
